TPU v7x, 32 devices: a whole 2x2x4 slice. The times are simulated.
32 devices in a mesh: ctx: 8 (over z, y), mp: 4 (over x, core).
Axes of the slice: x: 2, y: 2, z: 4, core: 2. Of those that a mesh axis runs over, the one named last changes fastest.
Arguments:
- q_mr: bfloat16 [2048, 4096], P('ctx', 'mp'), may hold values from -6 to 6
- k_mr: bfloat16 [2048, 4096], P('ctx', 'mp'), may hold values from -6 to 6
- v_mr: bfloat16 [2048, 4096], P('ctx', 'mp'), may hold values from -6 to 6
- q_li: bfloat16 [2048, 4096], P('ctx', 'mp'), may hold values from -6 to 6
- k_li: bfloat16 [2048, 4096], P('ctx', 'mp'), may hold values from -6 to 6
- short_taps: float32 [6, 3, 4096], P(None, None, 'mp'), may hold values from -3.5 to 3.5
- mr_taps: float32 [128, 4096], P(None, 'mp'), may hold values from -0.5 to 0.5
- norm_gain: float32 [4096], P('mp'), may hold values from 0.1 to 1.9
- decay_rate: float32 [16, 4096], P(None, 'mp'), may hold values from 0.00014648438 to 0.03
- residue: float32 [16, 4096], P(None, 'mp'), may hold values from -1.5 to 1.5
Outputs:
- mixer_mr: bfloat16 [2048, 4096], P('ctx', 'mp')
- mixer_li: bfloat16 [2048, 4096], P('ctx', 'mp')
All inputs are finite; a program needn't handle non-finite values.
Results may differ from a plain program's by a relative error of at most 0.0078.
Values may be sent and summed in bfloat16 or wider, within the bound.
A program may use at most 64 MiB of HBM per device.

v0:
```python
import jax
import jax.numpy as jnp
from jax import lax
from jax.sharding import PartitionSpec as P

D = 4096


def shifted(shard, axis, by):
    devices = lax.axis_size(axis)
    pairs = [(i, i + by) for i in range(devices) if 0 <= i + by < devices]
    return lax.ppermute(shard, axis, pairs)


def settle(values):
    return lax.optimization_barrier(values.astype(jnp.bfloat16))


def causal_conv(extended, taps):
    kernel = taps[::-1][:, None, :]
    return lax.conv_general_dilated(
        extended,
        kernel,
        (1,),
        "VALID",
        dimension_numbers=("NWC", "WIO", "NWC"),
        feature_group_count=taps.shape[1],
        precision=lax.Precision.HIGHEST,
    )


def extend_conv(rim, stream, taps):
    extended = jnp.concatenate([rim, stream], axis=0).astype(jnp.float32)[None]
    return causal_conv(extended, taps)[0]


def mode_weight(rate, res):
    return res * jnp.sqrt(-jnp.expm1(-2.0 * rate))


def carry_factor(rate_t, res_t, length):
    times = (jnp.arange(length) + 1).astype(jnp.float32)
    return mode_weight(rate_t, res_t)[:, :, None] * jnp.exp(
        -rate_t[:, :, None] * times[None, None, :]
    )


def inner_block(blocks, rate_g, res_g):
    width = blocks.shape[2]
    lag = jnp.arange(width)[:, None] - jnp.arange(width)[None, :]
    lagf = jnp.maximum(lag, 0).astype(jnp.float32)
    weight = mode_weight(rate_g, res_g)
    terms = weight[:, :, None, None] * jnp.exp(-rate_g[:, :, None, None] * lagf[None, None])
    toeplitz = jnp.where((lag >= 0)[None], jnp.sum(terms, axis=1), 0.0)
    return jnp.einsum("cbj,cij->cbi", blocks, toeplitz, precision=lax.Precision.HIGHEST)


def combine(earlier, later):
    return (earlier[0] * later[0], later[0] * earlier[1] + later[1])


def modal_long(values, rate, res):
    channels, length = values.shape
    width = 128
    count = length // width
    blocks = values.reshape(channels, count, width)
    rate_t = rate.T
    res_t = res.T
    group = min(channels, 16)
    groups = channels // group
    modes = rate_t.shape[1]

    def one_group(triple):
        return inner_block(triple[0], triple[1], triple[2])

    local = lax.map(
        one_group,
        (
            blocks.reshape(groups, group, count, width),
            rate_t.reshape(groups, group, modes),
            res_t.reshape(groups, group, modes),
        ),
    )
    local = local.reshape(channels, count, width)
    lags = (width - 1 - jnp.arange(width)).astype(jnp.float32)
    edge = jnp.exp(-rate_t[:, :, None] * lags[None, None, :])
    ends = jnp.einsum("cbj,cmj->cbm", blocks, edge, precision=lax.Precision.HIGHEST)
    decay = jnp.broadcast_to(jnp.exp(-rate_t * width)[:, None, :], ends.shape)
    _, inclusive = lax.associative_scan(combine, (decay, ends), axis=1)
    starts = jnp.concatenate([jnp.zeros_like(inclusive[:, :1]), inclusive[:, :-1]], axis=1)
    carried = jnp.einsum(
        "cbm,cmi->cbi", starts, carry_factor(rate_t, res_t, width), precision=lax.Precision.HIGHEST
    )
    return ((local + carried).reshape(channels, length), inclusive[:, -1])


def shards(q_mr, k_mr, v_mr, q_li, k_li, short_taps, mr_taps, norm_gain, decay_rate, residue):
    short_rim = short_taps.shape[1] - 1
    filt_rim = mr_taps.shape[0] - 1
    stacked = jnp.stack([q_mr[-short_rim:], q_li[-short_rim:], k_li[-short_rim:]])
    rims = shifted(stacked, "ctx", 1)
    depth = filt_rim + short_rim
    deep = shifted(jnp.stack([k_mr[-depth:], v_mr[-depth:]]), "ctx", 1)
    sq = extend_conv(rims[0], q_mr, short_taps[0])
    sk_ext = extend_conv(deep[0], k_mr, short_taps[1])
    sv_ext = extend_conv(deep[1], v_mr, short_taps[2])
    u_ext = settle(sk_ext * sv_ext)
    query_rim, key_rim = (rims[1], rims[2])
    mr_long = causal_conv(u_ext.astype(jnp.float32)[None], mr_taps)[0]
    mixer_mr = (sq * mr_long).astype(jnp.bfloat16)
    wide = mixer_mr.astype(jnp.float32)
    totals = lax.psum(jnp.sum(wide * wide, axis=1), "mp")
    normed = settle(wide * lax.rsqrt(totals / D + 1e-06)[:, None] * norm_gain[None, :])
    value_rim = shifted(normed[-short_rim:], "ctx", 1)
    lq = extend_conv(query_rim, q_li, short_taps[3])
    lk = extend_conv(key_rim, k_li, short_taps[4])
    lv = extend_conv(value_rim, normed, short_taps[5])
    u_li = settle(lk * lv)
    owned = lax.all_to_all(u_li.T, "ctx", split_axis=0, concat_axis=1, tiled=True)
    narrow = owned.shape[0]
    first = lax.axis_index("ctx") * narrow
    own_rate = lax.dynamic_slice_in_dim(decay_rate, first, narrow, 1)
    own_res = lax.dynamic_slice_in_dim(residue, first, narrow, 1)
    result, _ = modal_long(owned.astype(jnp.float32), own_rate, own_res)
    long_own = settle(result)
    long_li = lax.all_to_all(long_own, "ctx", split_axis=1, concat_axis=0, tiled=True).T
    mixer_li = (lq * long_li.astype(jnp.float32)).astype(jnp.bfloat16)
    return (mixer_mr, mixer_li)


def solution(mesh):
    in_specs = (
        P("ctx", "mp"),
        P("ctx", "mp"),
        P("ctx", "mp"),
        P("ctx", "mp"),
        P("ctx", "mp"),
        P(None, None, "mp"),
        P(None, "mp"),
        P("mp"),
        P(None, "mp"),
        P(None, "mp"),
    )
    out_specs = (P("ctx", "mp"), P("ctx", "mp"))
    return jax.shard_map(shards, mesh=mesh, in_specs=in_specs, out_specs=out_specs, check_vma=False)
```

profile of v0, /device:TPU:0, one launch (start us, length us, event | category | flops | bytes accessed | tf_op | source)
XLA Modules:
  0.0 160.4 jit_solution(17890497595315963001)
XLA Ops:
  3.3 4.9 %collective-permute-start.1 = (bf16[2,129,1024]{2,0,1:T(2,128)(2,1)}, bf16[2,129,1024]{2,0,1:T(2,128)(2,1)S(1)}, u32[]{:S(2)}, u32[]{:S(2)}) collective-permute-start(bf16[2,129,1024]{2,0,1:T(2,128)(2,1)} %copy.222), channel_id=1, source_target_pairs={{0,4},{4,8},{8,12},{12,16},{16,20},{20,24},{24,28},{1,5},{5,9},{9,... | collective-permute-start | bytes 1585160 | tf_op jit(solution)/shard_map/ppermute | solution.py:12
  9.0 3.4 %collective-permute-start = (bf16[3,2,1024]{2,1,0:T(2,128)(2,1)S(1)}, bf16[3,2,1024]{2,1,0:T(2,128)(2,1)S(1)}, u32[]{:S(2)}, u32[]{:S(2)}) collective-permute-start(bf16[3,2,1024]{2,1,0:T(2,128)(2,1)S(1)} %pad_maximum_fusion.4), channel_id=1, source_target_pairs={{0,4},{4,8},{8,12},{12,16},{16,20},{20,24},{24,28},{1,5},{5,9},{9,... | collective-permute-start | bytes 36872 | tf_op jit(solution)/shard_map/ppermute | solution.py:12
  12.4 2.4 %rev.22 = f32[3,1024]{1,0:T(4,128)} reverse(f32[3,1024]{1,0:T(4,128)S(1)} %get-tuple-element.56), dimensions={0} | reverse | bytes 24576 | tf_op jit(solution)/shard_map/rev | solution.py:20
  15.3 2.6 %rev.24 = f32[128,1024]{1,0:T(8,128)} reverse(f32[128,1024]{1,0:T(8,128)S(1)} %copy-done.10), dimensions={0} | reverse | bytes 1048576 | tf_op jit(solution)/shard_map/rev | solution.py:20
  31.5 11.1 %fusion.23 = bf16[1,256,1024]{2,0,1:T(2,128)(2,1)S(1)} fusion(bf16[1,383,1024]{2,1,0:T(8,128)(2,1)S(1)} %bitcast.147, f32[1,264,1024]{2,0,1:T(1,128)S(1)} %reshape.169, f32[128,1,1024]{2,0,1:T(8,128)S(1)} %bitcast.148), kind=kOutput, calls=%fused_computation.37 | convolution fusion | flops 403177472 | bytes 2881536 | tf_op jit(solution)/shard_map/conv_general_dilated | solution.py:21
  42.8 5.7 %psum.7 = f32[256]{0:T(256)S(1)} all-reduce(f32[256]{0:T(256)S(1)} %get-tuple-element.48), channel_id=1, replica_groups=mesh['ctx'=8,'mp'=4] {'mp'}, use_global_device_ids=true, to_apply=%region_1.0 | all-reduce | flops 256 | bytes 2048 | tf_op jit(solution)/shard_map/psum | solution.py:112
  48.8 4.6 %collective-permute-start.2 = (bf16[2,1024]{1,0:T(2,128)(2,1)S(1)}, bf16[2,1024]{1,0:T(2,128)(2,1)S(1)}, u32[]{:S(2)}, u32[]{:S(2)}) collective-permute-start(bf16[2,1024]{1,0:T(2,128)(2,1)S(1)} %slice.198), channel_id=1, source_target_pairs={{0,4},{4,8},{8,12},{12,16},{16,20},{20,24},{24,28},{1,5},{5,9},{9,... | collective-permute-start | bytes 12296 | tf_op jit(solution)/shard_map/ppermute | solution.py:12
  57.1 7.4 %all-to-all-start = ((bf16[8,128,256]{2,1,0:T(8,128)(2,1)}), bf16[8,128,256]{2,1,0:T(8,128)(2,1)S(1)}, u32[]{:S(2)}, u32[]{:S(2)}) async-start(bf16[8,128,256]{2,1,0:T(8,128)(2,1)} %bitcast.44), calls=%async_computation | async-start | bytes 1048576 | tf_op jit(solution)/shard_map/all_to_all | solution.py:119
  65.7 12.1 %all-to-all-done = bf16[8,128,256]{2,1,0:T(8,128)(2,1)S(1)} async-done(((bf16[8,128,256]{2,1,0:T(8,128)(2,1)}), bf16[8,128,256]{2,1,0:T(8,128)(2,1)S(1)}, u32[]{:S(2)}, u32[]{:S(2)}) %all-to-all-start) | async-done | bytes 524320 | tf_op jit(solution)/shard_map/all_to_all | solution.py:119
  84.0 54.1 %while.10 = (s32[]{:T(128)}, f32[8,16,16,128]{3,2,1,0:T(8,128)}, f32[8,16,16,128]{3,2,1,0:T(8,128)S(1)}, f32[8,16,16]{2,1,0:T(8,128)S(1)}, f32[8,16,16]{2,1,0:T(8,128)S(1)}, /*index=5*/s32[]{:T(128)}) while((s32[]{:T(128)}, f32[8,16,16,128]{3,2,1,0:T(8,128)}, f32[8,16,16,128]{3,2,1,0:T(8,128)S(1)}, f32[8,16,16]{2,1,0:T(8,128)S(1)}, ...), condition=%wide.region_4.5_spmd, body=%wide.region_2.4_spmd.sunk | while | flops 62997504 | bytes 2530377 | solution.py:76
  84.1 4.3 %multiply_reduce_fusion.2 = f32[16,128,128]{2,1,0:T(8,128)S(1)} fusion(f32[128,128]{1,0:T(8,128)S(1)} %maximum_convert_fusion.2, f32[16,16]{1,0:T(8,128)S(1)} %get-tuple-element.108, f32[16,16]{1,0:T(8,128)S(1)} %get-tuple-element.109), kind=kLoop, calls=%fused_computation.clone.1 | loop fusion | flops 12320768 | bytes 1116160 | tf_op jit(solution)/shard_map/while/body/eval_jaxpr/reduce_sum | solution.py:54
  88.4 2.4 %fusion.129 = f32[8,16,16,128]{3,2,1,0:T(8,128)} fusion(f32[8,16,16,128]{3,2,1,0:T(8,128)} %get-tuple-element.117, s32[]{:T(128)} %get-tuple-element.116, f32[16,128,128]{2,1,0:T(8,128)S(1)} %multiply_reduce_fusion.2, pred[128,128]{1,0:T(8,128)(4,1)S(1)} %fusion.128, f32[8,16,16,128]{3,2,1,0:T(8,128)S(1)} %get-tuple-element.124), kind=kOutput, calls=%fused_computation.2.clone.1 | convolution fusion | flops 50593792 | bytes 1328128 | tf_op jit(solution)/shard_map/while/body/eval_jaxpr/cbj,cij->cbi/dot_general | solution.py:55
  90.9 4.3 %multiply_reduce_fusion.2 = f32[16,128,128]{2,1,0:T(8,128)S(1)} fusion(f32[128,128]{1,0:T(8,128)S(1)} %maximum_convert_fusion.2, f32[16,16]{1,0:T(8,128)S(1)} %get-tuple-element.108, f32[16,16]{1,0:T(8,128)S(1)} %get-tuple-element.109), kind=kLoop, calls=%fused_computation.clone.1 | loop fusion | flops 12320768 | bytes 1116160 | tf_op jit(solution)/shard_map/while/body/eval_jaxpr/reduce_sum | solution.py:54
  97.6 4.3 %multiply_reduce_fusion.2 = f32[16,128,128]{2,1,0:T(8,128)S(1)} fusion(f32[128,128]{1,0:T(8,128)S(1)} %maximum_convert_fusion.2, f32[16,16]{1,0:T(8,128)S(1)} %get-tuple-element.108, f32[16,16]{1,0:T(8,128)S(1)} %get-tuple-element.109), kind=kLoop, calls=%fused_computation.clone.1 | loop fusion | flops 12320768 | bytes 1116160 | tf_op jit(solution)/shard_map/while/body/eval_jaxpr/reduce_sum | solution.py:54
  104.4 4.3 %multiply_reduce_fusion.2 = f32[16,128,128]{2,1,0:T(8,128)S(1)} fusion(f32[128,128]{1,0:T(8,128)S(1)} %maximum_convert_fusion.2, f32[16,16]{1,0:T(8,128)S(1)} %get-tuple-element.108, f32[16,16]{1,0:T(8,128)S(1)} %get-tuple-element.109), kind=kLoop, calls=%fused_computation.clone.1 | loop fusion | flops 12320768 | bytes 1116160 | tf_op jit(solution)/shard_map/while/body/eval_jaxpr/reduce_sum | solution.py:54
  111.1 4.3 %multiply_reduce_fusion.2 = f32[16,128,128]{2,1,0:T(8,128)S(1)} fusion(f32[128,128]{1,0:T(8,128)S(1)} %maximum_convert_fusion.2, f32[16,16]{1,0:T(8,128)S(1)} %get-tuple-element.108, f32[16,16]{1,0:T(8,128)S(1)} %get-tuple-element.109), kind=kLoop, calls=%fused_computation.clone.1 | loop fusion | flops 12320768 | bytes 1116160 | tf_op jit(solution)/shard_map/while/body/eval_jaxpr/reduce_sum | solution.py:54
  115.5 2.4 %fusion.129 = f32[8,16,16,128]{3,2,1,0:T(8,128)} fusion(f32[8,16,16,128]{3,2,1,0:T(8,128)} %get-tuple-element.117, s32[]{:T(128)} %get-tuple-element.116, f32[16,128,128]{2,1,0:T(8,128)S(1)} %multiply_reduce_fusion.2, pred[128,128]{1,0:T(8,128)(4,1)S(1)} %fusion.128, f32[8,16,16,128]{3,2,1,0:T(8,128)S(1)} %get-tuple-element.124), kind=kOutput, calls=%fused_computation.2.clone.1 | convolution fusion | flops 50593792 | bytes 1328128 | tf_op jit(solution)/shard_map/while/body/eval_jaxpr/cbj,cij->cbi/dot_general | solution.py:55
  117.9 4.3 %multiply_reduce_fusion.2 = f32[16,128,128]{2,1,0:T(8,128)S(1)} fusion(f32[128,128]{1,0:T(8,128)S(1)} %maximum_convert_fusion.2, f32[16,16]{1,0:T(8,128)S(1)} %get-tuple-element.108, f32[16,16]{1,0:T(8,128)S(1)} %get-tuple-element.109), kind=kLoop, calls=%fused_computation.clone.1 | loop fusion | flops 12320768 | bytes 1116160 | tf_op jit(solution)/shard_map/while/body/eval_jaxpr/reduce_sum | solution.py:54
  124.7 4.3 %multiply_reduce_fusion.2 = f32[16,128,128]{2,1,0:T(8,128)S(1)} fusion(f32[128,128]{1,0:T(8,128)S(1)} %maximum_convert_fusion.2, f32[16,16]{1,0:T(8,128)S(1)} %get-tuple-element.108, f32[16,16]{1,0:T(8,128)S(1)} %get-tuple-element.109), kind=kLoop, calls=%fused_computation.clone.1 | loop fusion | flops 12320768 | bytes 1116160 | tf_op jit(solution)/shard_map/while/body/eval_jaxpr/reduce_sum | solution.py:54
  131.4 4.3 %multiply_reduce_fusion.2 = f32[16,128,128]{2,1,0:T(8,128)S(1)} fusion(f32[128,128]{1,0:T(8,128)S(1)} %maximum_convert_fusion.2, f32[16,16]{1,0:T(8,128)S(1)} %get-tuple-element.108, f32[16,16]{1,0:T(8,128)S(1)} %get-tuple-element.109), kind=kLoop, calls=%fused_computation.clone.1 | loop fusion | flops 12320768 | bytes 1116160 | tf_op jit(solution)/shard_map/while/body/eval_jaxpr/reduce_sum | solution.py:54
  135.7 2.4 %fusion.129 = f32[8,16,16,128]{3,2,1,0:T(8,128)} fusion(f32[8,16,16,128]{3,2,1,0:T(8,128)} %get-tuple-element.117, s32[]{:T(128)} %get-tuple-element.116, f32[16,128,128]{2,1,0:T(8,128)S(1)} %multiply_reduce_fusion.2, pred[128,128]{1,0:T(8,128)(4,1)S(1)} %fusion.128, f32[8,16,16,128]{3,2,1,0:T(8,128)S(1)} %get-tuple-element.124), kind=kOutput, calls=%fused_computation.2.clone.1 | convolution fusion | flops 50593792 | bytes 1328128 | tf_op jit(solution)/shard_map/while/body/eval_jaxpr/cbj,cij->cbi/dot_general | solution.py:55
  138.1 2.7 %fusion.15 = bf16[128,16,128]{2,1,0:T(8,128)(2,1)S(1)} fusion(f32[128,16,128]{2,1,0:T(8,128)} %bitcast.50, f32[128,15,16]{2,1,0:T(8,128)S(1)} %copy.268, f32[128]{0:T(128)S(1)} %add_convert_fusion, f32[128,16]{1,0:T(8,128)S(1)} %copy.255, f32[128,16]{1,0:T(8,128)S(1)} %copy.250), kind=kOutput, calls=%fused_computation.30 | convolution fusion | flops 51380224 | bytes 1712640 | tf_op jit(solution)/shard_map/cbm,cmi->cbi/dot_general | solution.py:91
  142.0 3.7 %all-to-all-start.1 = ((bf16[128,8,256]{0,2,1:T(8,128)(2,1)}), bf16[128,8,256]{0,2,1:T(8,128)(2,1)S(1)}, u32[]{:S(2)}, u32[]{:S(2)}) async-start(bf16[128,8,256]{0,2,1:T(8,128)(2,1)} %bitcast.53), calls=%async_computation.1 | async-start | bytes 1048576 | tf_op jit(solution)/shard_map/all_to_all | solution.py:126
  147.7 11.8 %all-to-all-done.1 = bf16[128,8,256]{0,2,1:T(8,128)(2,1)S(1)} async-done(((bf16[128,8,256]{0,2,1:T(8,128)(2,1)}), bf16[128,8,256]{0,2,1:T(8,128)(2,1)S(1)}, u32[]{:S(2)}, u32[]{:S(2)}) %all-to-all-start.1) | async-done | bytes 524320 | tf_op jit(solution)/shard_map/all_to_all | solution.py:126
  (183 shorter events, 44.6 us)
Async XLA Ops:
  1.8 6.4 %copy-start.7 = (bf16[256,1024]{1,0:T(8,128)(2,1)S(1)}, bf16[256,1024]{1,0:T(8,128)(2,1)}, u32[]{:S(2)}) copy-start(bf16[256,1024]{1,0:T(8,128)(2,1)} %param.12) | copy-start | bytes 1572868
  1.8 6.4 %copy-start.8 = (bf16[256,1024]{1,0:T(8,128)(2,1)S(1)}, bf16[256,1024]{1,0:T(8,128)(2,1)}, u32[]{:S(2)}) copy-start(bf16[256,1024]{1,0:T(8,128)(2,1)} %param.16) | copy-start | bytes 1572868
  1.8 10.6 %copy-start.12 = (f32[6,3,1024]{2,1,0:T(4,128)S(1)}, f32[6,3,1024]{2,1,0:T(4,128)}, u32[]{:S(2)}) copy-start(f32[6,3,1024]{2,1,0:T(4,128)} %param.17) | copy-start | bytes 221188
  1.8 13.4 %copy-start.10 = (f32[128,1024]{1,0:T(8,128)S(1)}, f32[128,1024]{1,0:T(8,128)}, u32[]{:S(2)}) copy-start(f32[128,1024]{1,0:T(8,128)} %param.18) | copy-start | bytes 1572868
  3.3 20.5 %collective-permute-start.1 = (bf16[2,129,1024]{2,0,1:T(2,128)(2,1)}, bf16[2,129,1024]{2,0,1:T(2,128)(2,1)S(1)}, u32[]{:S(2)}, u32[]{:S(2)}) collective-permute-start(bf16[2,129,1024]{2,0,1:T(2,128)(2,1)} %copy.222), channel_id=1, source_target_pairs={{0,4},{4,8},{8,12},{12,16},{16,20},{20,24},{24,28},{1,5},{5,9},{9,... | collective-permute-start | bytes 1585160 | tf_op jit(solution)/shard_map/ppermute | solution.py:12
  9.0 10.9 %collective-permute-start = (bf16[3,2,1024]{2,1,0:T(2,128)(2,1)S(1)}, bf16[3,2,1024]{2,1,0:T(2,128)(2,1)S(1)}, u32[]{:S(2)}, u32[]{:S(2)}) collective-permute-start(bf16[3,2,1024]{2,1,0:T(2,128)(2,1)S(1)} %pad_maximum_fusion.4), channel_id=1, source_target_pairs={{0,4},{4,8},{8,12},{12,16},{16,20},{20,24},{24,28},{1,5},{5,9},{9,... | collective-permute-start | bytes 36872 | tf_op jit(solution)/shard_map/ppermute | solution.py:12
  20.1 0.7 copy-start.16
  23.7 0.9 copy-start.5
  23.7 1.2 copy-start.1
  25.4 1.4 copy-start.2
  25.9 0.9 copy-start.3
  27.3 1.1 copy-start.4
  27.3 1.1 copy-start.13
  28.4 0.7 copy-start.15
  30.4 1.0 copy-start.11
  42.5 6.0 %copy-start.14 = (f32[1024]{0:T(1024)S(1)}, f32[1024]{0:T(1024)}, u32[]{:S(2)}) copy-start(f32[1024]{0:T(1024)} %param.19) | copy-start | bytes 12292
  42.6 10.8 %copy-start.6 = (bf16[1,8,33,1024]{3,1,2,0:T(8,128)(2,1)S(1)}, bf16[1,8,33,1024]{3,1,2,0:T(8,128)(2,1)}, u32[]{:S(2)}) copy-start(bf16[1,8,33,1024]{3,1,2,0:T(8,128)(2,1)} %copy-done.5) | copy-start | bytes 1622020
  42.6 10.8 %copy-start.17 = (pred[8,33]{0,1:T(8,128)(4,1)S(1)}, pred[8,33]{0,1:T(8,128)(4,1)}, u32[]{:S(2)}) copy-start(pred[8,33]{0,1:T(8,128)(4,1)} %constant.102) | copy-start | bytes 796
  42.8 10.8 %copy-start = (bf16[256,1024]{1,0:T(8,128)(2,1)}, bf16[256,1024]{1,0:T(8,128)(2,1)S(1)}, u32[]{:S(2)}) copy-start(bf16[256,1024]{1,0:T(8,128)(2,1)S(1)} %get-tuple-element.49) | copy-start | bytes 1572868
  48.8 5.7 %collective-permute-start.2 = (bf16[2,1024]{1,0:T(2,128)(2,1)S(1)}, bf16[2,1024]{1,0:T(2,128)(2,1)S(1)}, u32[]{:S(2)}, u32[]{:S(2)}) collective-permute-start(bf16[2,1024]{1,0:T(2,128)(2,1)S(1)} %slice.198), channel_id=1, source_target_pairs={{0,4},{4,8},{8,12},{12,16},{16,20},{20,24},{24,28},{1,5},{5,9},{9,... | collective-permute-start | bytes 12296 | tf_op jit(solution)/shard_map/ppermute | solution.py:12
  57.1 20.8 %all-to-all-start = ((bf16[8,128,256]{2,1,0:T(8,128)(2,1)}), bf16[8,128,256]{2,1,0:T(8,128)(2,1)S(1)}, u32[]{:S(2)}, u32[]{:S(2)}) async-start(bf16[8,128,256]{2,1,0:T(8,128)(2,1)} %bitcast.44), calls=%async_computation | async-start | bytes 1048576 | tf_op jit(solution)/shard_map/all_to_all | solution.py:119
  141.0 4.9 %copy-start.9 = (bf16[256,1024]{1,0:T(8,128)(2,1)S(1)}, bf16[256,1024]{1,0:T(8,128)(2,1)}, u32[]{:S(2)}) copy-start(bf16[256,1024]{1,0:T(8,128)(2,1)} %param.15) | copy-start | bytes 1572868
  142.0 17.5 %all-to-all-start.1 = ((bf16[128,8,256]{0,2,1:T(8,128)(2,1)}), bf16[128,8,256]{0,2,1:T(8,128)(2,1)S(1)}, u32[]{:S(2)}, u32[]{:S(2)}) async-start(bf16[128,8,256]{0,2,1:T(8,128)(2,1)} %bitcast.53), calls=%async_computation.1 | async-start | bytes 1048576 | tf_op jit(solution)/shard_map/all_to_all | solution.py:126
where the time goes:
time: 161 us; the launch traced here: 160 us
  other arithmetic  38 us (24%)
  matrix products  36.3 us (23%)
  local copies, waits for them, and re-layouts  28.4 us (18%)
  waiting for transfers between devices  26.2 us (16%)
  starting transfers between devices  24 us (15%)
  blocking collectives  5.72 us (4%)
    reduce_sum x8, other arithmetic, inner_block(): toeplitz = jnp.where((lag >= 0)[None], jnp.sum(terms, axis=1), 0.0)  34.3 us
    dot_general x8, matrix products, inner_block(): jnp.einsum('cbj,cij->cbi', blocks, toeplitz, precision=lax.Precision.HIGH...  19.2 us
    conv_general_dilated x7, matrix products, causal_conv(): lax.conv_general_dilated(extended, kernel, (1,), 'VALID', dimension_numbe...  13.4 us
    ppermute x3, starting transfers between devices, shifted(): return lax.ppermute(shard, axis, pairs)  12.9 us
    all_to_all x1, waiting for transfers between devices, shards(): lax.all_to_all(u_li.T, 'ctx', split_axis=0, concat_axis=1, tiled=True)  12.1 us
    all_to_all x1, waiting for transfers between devices, shards(): lax.all_to_all(long_own, 'ctx', split_axis=1, concat_axis=0, tiled=True)  11.8 us
    all_to_all x1, starting transfers between devices, shards(): lax.all_to_all(u_li.T, 'ctx', split_axis=0, concat_axis=1, tiled=True)  7.44 us
    conv_general_dilated x22, local copies, waits for them, and re-layouts, causal_conv(): lax.conv_general_dilated(extended, kernel, (1,), 'VALID', dimension_numbe...  6.17 us
  transfers between devices with their start and end apart: 5, of which 4 were waited for; matrix products, arithmetic and copies ran while one was open for 8% of the time, Pallas kernels for 0%

commit v1 on v0

v1 whole, which is shorter than its diff:
```python
import functools

import jax
import jax.numpy as jnp
import numpy as np
from jax import lax
from jax.experimental import pallas as pl
from jax.experimental.pallas import tpu as pltpu
from jax.sharding import PartitionSpec as P

MESH = pl.DeviceIdType.MESH
BF = jnp.bfloat16
F32 = jnp.float32


def two_parts(m):
    hi = np.asarray(m, np.float32).astype(BF)
    lo = (np.asarray(m, np.float64) - hi.astype(np.float64)).astype(BF)
    return hi, lo


def dft_tables(length, first_out, n_in):
    half = length // 2
    k = np.arange(half)[:, None]
    t = np.arange(length)[None, :]
    ang = 2 * np.pi * ((k * t) % length) / length
    cos, sin = np.cos(ang), -np.sin(ang)
    sin[0] = (-1.0) ** np.arange(length)
    forward = np.concatenate([cos, sin], 0)
    wc, ws = 2 * cos, 2 * sin
    wc[0] = 1.0
    ws[0] = (-1.0) ** np.arange(length)
    inverse = np.concatenate([wc, ws], 0).T / length
    return two_parts(forward[:, :n_in]), two_parts(inverse[first_out:])


def dot(a, b):
    return jnp.dot(a, b, preferred_element_type=F32)


def split(x):
    hi = x.astype(BF)
    return hi, (x - hi.astype(F32)).astype(BF)


def dot3(ah, al, x):
    hi, lo = split(x)
    return dot(ah, hi) + dot(ah, lo) + dot(al, hi)


def conv3(x, rim8, taps):
    ext = jnp.concatenate([rim8, x], axis=0)
    x1 = pltpu.roll(ext, 1, 0)[8:]
    x2 = pltpu.roll(ext, 2, 0)[8:]
    return taps[0:1] * x + taps[1:2] * x1 + taps[2:3] * x2


def spectrum_product(u, h, half):
    ur, ui = u[:half], u[half:]
    hr, hi, hn = h[:half], h[half : 2 * half], h[2 * half :]
    hr2 = jnp.concatenate([hn, hr[8:]], axis=0)
    return jnp.concatenate([ur * hr - ui * hi, ur * hi + ui * hr2], axis=0)


def store_spectrum(ref, h, half, cols):
    top = lax.broadcasted_iota(jnp.int32, (8, h.shape[1]), 0) == 0
    hr, hi = h[:half], h[half:]
    ref[0:half, cols] = hr
    ref[half : half + 8, cols] = jnp.where(top, 0.0, hi[:8])
    ref[half + 8 : 2 * half, cols] = hi[8:]
    ref[2 * half : 2 * half + 8, cols] = jnp.where(top, hi[:8], hr[:8])


def kernel(
    n, mp, q_mr, k_mr, v_mr, q_li, k_li, short, mr_taps, gain, rate, res, f1h, f1l, g1h, g1l, f2h, f2l, g2h, g2l,
    out_mr, out_li,
    u_own, u_halo, pack, rims, spec1, spec2, hbuf, lkb, lqb, nbuf, nrim, u32, ylong, wgt, ebuf, carry, st, ss, scale, acc_ss,
    rim_s, rim_r, halo_s, halo_r, nr_s, nr_r, ss_s, ss_r, st_s, st_r,
):
    T, C = q_mr.shape
    H = T // 2
    modes = rate.shape[0]
    CW = 256
    chunks = C // CW
    ctx = lax.axis_index("ctx")
    mpi = lax.axis_index("mp")
    not_last = ctx < n - 1
    not_first = ctx > 0

    def cols_of(i, w=CW):
        return pl.ds(pl.multiple_of(i * w, w), w)

    def loop(count, body):
        def step(i, c):
            body(i)
            return c

        lax.fori_loop(0, count, step, 0)

    barrier = pltpu.get_barrier_semaphore()

    def greet(j, c):
        pl.semaphore_signal(barrier, inc=1, device_id={"ctx": lax.rem(ctx + j, n)}, device_id_type=MESH)
        return c

    lax.fori_loop(1, n, greet, 0)
    for j in range(1, mp):
        pl.semaphore_signal(barrier, inc=1, device_id={"mp": lax.rem(mpi + j, mp)}, device_id_type=MESH)

    def pack_body(i):
        cols = cols_of(i)
        row = lax.broadcasted_iota(jnp.int32, (8, CW), 0)
        first = jnp.zeros((8, CW), F32)
        second = jnp.zeros((8, CW), F32)
        for s, stream in enumerate((q_mr, k_mr, v_mr, q_li, k_li)):
            tail = stream[T - 16 : T, cols].astype(F32)[8:]
            moved = pltpu.roll(tail, (2 + 2 * s) % 8, 0) if (2 + 2 * s) % 8 else tail
            here = (row >= (2 * s) % 8) & (row < (2 * s) % 8 + 2)
            if s < 4:
                first = jnp.where(here, moved, first)
            else:
                second = jnp.where(here, moved, second)
        pack[:, cols] = jnp.concatenate([first, second], axis=0).astype(BF)

    loop(chunks, pack_body)

    @pl.when(jnp.logical_not(not_first))
    def _():
        rims[...] = jnp.zeros(rims.shape, BF)
        nrim[...] = jnp.zeros(nrim.shape, BF)
        u_halo[...] = jnp.zeros(u_halo.shape, BF)

    def u_rows(lo, rows, cols, rim_k, rim_v):
        k = conv3(k_mr[lo : lo + rows, cols].astype(F32), rim_k, short[1, :, cols])
        v = conv3(v_mr[lo : lo + rows, cols].astype(F32), rim_v, short[2, :, cols])
        u_own[lo : lo + rows, cols] = (k * v).astype(BF)

    def before(stream, lo, cols):
        return stream[lo - 16 : lo, cols].astype(F32)[8:]

    def u_late(i):
        cols = cols_of(i)
        u_rows(H, H, cols, before(k_mr, H, cols), before(v_mr, H, cols))

    loop(chunks, u_late)

    pl.semaphore_wait(barrier, n - 1 + mp - 1)

    nxt = {"ctx": lax.rem(ctx + 1, n)}
    rim_copy = pltpu.make_async_remote_copy(pack, rims, rim_s, rim_r, device_id=nxt, device_id_type=MESH)
    halo_copy = pltpu.make_async_remote_copy(
        u_own.at[pl.ds(H, H)], u_halo, halo_s, halo_r, device_id=nxt, device_id_type=MESH
    )
    nr_copy = pltpu.make_async_remote_copy(
        nbuf.at[pl.ds(T - 16, 16)], nrim, nr_s, nr_r, device_id=nxt, device_id_type=MESH
    )

    @pl.when(not_last)
    def _():
        rim_copy.start()
        halo_copy.start()

    def mr_spec(i):
        cols = cols_of(i)
        store_spectrum(spec1, dot3(f1h[:, 0:H], f1l[:, 0:H], mr_taps[:, cols]), T // 2, cols)

    loop(chunks, mr_spec)

    @pl.when(not_first)
    def _():
        rim_copy.wait_recv()

    def rim_of(s, cols):
        both = rims[:, cols].astype(F32)
        part = both[0:8] if s < 4 else both[8:16]
        by = (6 - 2 * s) % 8
        return pltpu.roll(part, by, 0) if by else part

    def u_early(i):
        cols = cols_of(i)
        u_rows(0, H, cols, rim_of(1, cols), rim_of(2, cols))

    loop(chunks, u_early)

    def mr_half(part):
        acc_ss[...] = jnp.zeros(acc_ss.shape, F32)

        def body(i):
            cols = cols_of(i)
            if part == 1:
                win = u_own[:, cols]
                sq = conv3(q_mr[H:T, cols].astype(F32), before(q_mr, H, cols), short[0, :, cols])
            else:
                win = jnp.concatenate([u_halo[:, cols], u_own[0:H, cols]], axis=0)
                sq = conv3(q_mr[0:H, cols].astype(F32), rim_of(0, cols), short[0, :, cols])
            u = dot(f1h[...], win) + dot(f1l[...], win)
            y = dot3(g1h[...], g1l[...], spectrum_product(u, spec1[:, cols], T // 2))
            m = (sq * y).astype(BF)
            out_mr[part * H : part * H + H, cols] = m
            w = m.astype(F32)
            w = w * w
            acc_ss[...] += w[:, 0:128] + w[:, 128:256]

        loop(chunks, body)
        row = jnp.sum(acc_ss[...].T, axis=0, keepdims=True)
        ss[part, mpi] = jnp.broadcast_to(row, (8, H))

    def ss_copy(part, j, slot):
        return pltpu.make_async_remote_copy(
            ss.at[part, slot], ss.at[part, slot], ss_s.at[part, j], ss_r.at[part, slot],
            device_id={"mp": lax.rem(mpi + j, mp)}, device_id_type=MESH,
        )

    def ss_send(part):
        for j in range(1, mp):
            ss_copy(part, j, mpi).start()

    def norm_half(part):
        for j in range(1, mp):
            ss_copy(part, j, lax.rem(mpi + j, mp)).wait_recv()
        total = ss[part, 0]
        for j in range(1, mp):
            total = total + ss[part, j]
        sc = lax.rsqrt(total / (C * mp) + 1e-06)
        scale[...] = jnp.broadcast_to(sc[0:1], (H, H)).T

        def body(i):
            cols = cols_of(i)
            s = scale[...]
            s = jnp.concatenate([s, s], axis=1)
            m = out_mr[part * H : part * H + H, cols].astype(F32)
            nbuf[part * H : part * H + H, cols] = (m * s * gain[0:1, cols]).astype(BF)

        loop(chunks, body)

    mr_half(1)
    ss_send(1)

    def li_gates(i):
        cols = cols_of(i)
        lkb[:, cols] = conv3(k_li[:, cols].astype(F32), rim_of(4, cols), short[4, :, cols])
        lqb[:, cols] = conv3(q_li[:, cols].astype(F32), rim_of(3, cols), short[3, :, cols])

    loop(chunks, li_gates)

    norm_half(1)

    @pl.when(not_last)
    def _():
        nr_copy.start()

    x = 2.0 * rate[...]
    series = x * (1.0 + x * (-1.0 / 2 + x * (1.0 / 6 + x * (-1.0 / 24 + x * (1.0 / 120 - x * (1.0 / 720))))))
    wgt[...] = res[...] * jnp.sqrt(jnp.where(x < 0.125, series, 1.0 - jnp.exp(-x)))

    sub = lax.broadcasted_iota(jnp.int32, (8, 128), 0).astype(F32)

    def rows_of(ref, cols):
        return [jnp.broadcast_to(ref[m : m + 1, cols], (8, 128)) for m in range(modes)]

    def tree(vals):
        vals = list(vals)
        while len(vals) > 1:
            vals = [a + b for a, b in zip(vals[0::2], vals[1::2])] + ([vals[-1]] if len(vals) % 2 else [])
        return vals[0]

    def h_group(i):
        cols = cols_of(i, 128)
        r = rows_of(rate, cols)
        w = rows_of(wgt, cols)
        d8 = [jnp.exp(-8.0 * a) for a in r]
        g = tuple(b * jnp.exp(-a * sub) for a, b in zip(r, w))

        def step(k, g):
            hbuf[pl.ds(pl.multiple_of(k * 8, 8), 8), cols] = tree(g)
            return tuple(a * b for a, b in zip(g, d8))

        lax.fori_loop(0, T // 8, step, g, unroll=4)

    loop(C // 128, h_group)

    def li_spec(i):
        cols = cols_of(i)
        store_spectrum(spec2, dot3(f2h[...], f2l[...], hbuf[:, cols]), T, cols)

    loop(chunks, li_spec)

    @pl.when(not_first)
    def _():
        halo_copy.wait_recv()

    mr_half(0)
    ss_send(0)
    norm_half(0)

    @pl.when(not_first)
    def _():
        nr_copy.wait_recv()

    def li_u(i):
        cols = cols_of(i)
        lv = conv3(nbuf[:, cols].astype(F32), nrim[:, cols].astype(F32)[8:], short[5, :, cols])
        u32[:, cols] = (lkb[:, cols] * lv).astype(BF).astype(F32)

    loop(chunks, li_u)

    def ends_group(i):
        cols = cols_of(i, 128)
        r = rows_of(rate, cols)
        d8 = [jnp.exp(-8.0 * a) for a in r]

        def step(k, acc):
            u = u32[pl.ds(pl.multiple_of(k * 8, 8), 8), cols]
            return tuple(a * d + u for a, d in zip(acc, d8))

        acc = lax.fori_loop(0, T // 8, step, tuple(jnp.zeros((8, 128), F32) for _ in r), unroll=4)
        for m in range(modes):
            ebuf[m : m + 1, cols] = jnp.sum(acc[m] * jnp.exp(-r[m] * (7.0 - sub)), axis=0, keepdims=True)

    loop(C // 128, ends_group)
    st[ctx] = ebuf[...].astype(BF)

    def st_copy(dst, slot):
        return pltpu.make_async_remote_copy(
            st.at[slot], st.at[slot], st_s.at[dst], st_r.at[slot], device_id={"ctx": dst}, device_id_type=MESH
        )

    def st_start(j, c):
        st_copy(j, ctx).start()
        return c

    lax.fori_loop(ctx + 1, n, st_start, 0)

    def li_local(i):
        cols = cols_of(i)
        win = u32[:, cols].astype(BF)
        u = dot(f2h[...], win) + dot(f2l[...], win)
        ylong[:, cols] = dot3(g2h[...], g2l[...], spectrum_product(u, spec2[:, cols], T))

    loop(chunks, li_local)

    carry[...] = jnp.zeros(carry.shape, F32)

    def st_take(j, c):
        st_copy(lax.rem(ctx + 1, n), j).wait_recv()
        carry[...] = carry[...] * jnp.exp(-float(T) * rate[...]) + st[j].astype(F32)
        return c

    lax.fori_loop(0, ctx, st_take, 0)

    def out_group(i):
        cols = cols_of(i, 128)
        r = rows_of(rate, cols)
        w = rows_of(wgt, cols)
        s = rows_of(carry, cols)
        d8 = [jnp.exp(-8.0 * a) for a in r]
        g = tuple(b * c * jnp.exp(-a * (sub + 1.0)) for a, b, c in zip(r, w, s))

        def step(k, g):
            rows = pl.ds(pl.multiple_of(k * 16, 16), 16)
            y0 = tree(g)
            g = tuple(a * b for a, b in zip(g, d8))
            y1 = tree(g)
            g = tuple(a * b for a, b in zip(g, d8))
            y = ylong[rows, cols] + jnp.concatenate([y0, y1], axis=0)
            out_li[rows, cols] = (lqb[rows, cols] * y.astype(BF).astype(F32)).astype(BF)
            return g

        lax.fori_loop(0, T // 16, step, g, unroll=2)

    loop(C // 128, out_group)

    @pl.when(not_last)
    def _():
        rim_copy.wait_send()
        halo_copy.wait_send()
        nr_copy.wait_send()

    for part in range(2):
        for j in range(1, mp):
            ss_copy(part, j, mpi).wait_send()

    def st_end(j, c):
        st_copy(j, ctx).wait_send()
        return c

    lax.fori_loop(ctx + 1, n, st_end, 0)


def shards(n, mp, q_mr, k_mr, v_mr, q_li, k_li, short_taps, mr_taps, norm_gain, decay_rate, residue):
    T, C = q_mr.shape
    modes = decay_rate.shape[0]
    (f1h, f1l), (g1h, g1l) = dft_tables(T, T // 2, T)
    (f2h, f2l), (g2h, g2l) = dft_tables(2 * T, 0, T)
    g2h, g2l = g2h[:T], g2l[:T]
    tables = [jnp.asarray(a) for a in (f1h, f1l, g1h, g1l, f2h, f2l, g2h, g2l)]
    vm = pl.BlockSpec(memory_space=pltpu.VMEM)
    DMA = pltpu.SemaphoreType.DMA
    H = T // 2
    return pl.pallas_call(
        functools.partial(kernel, n, mp),
        out_shape=(jax.ShapeDtypeStruct((T, C), BF), jax.ShapeDtypeStruct((T, C), BF)),
        in_specs=[vm] * 18,
        out_specs=(vm, vm),
        scratch_shapes=[
            pltpu.VMEM((T, C), BF),
            pltpu.VMEM((H, C), BF),
            pltpu.VMEM((16, C), BF),
            pltpu.VMEM((16, C), BF),
            pltpu.VMEM((T + 8, C), F32),
            pltpu.VMEM((2 * T + 8, C), F32),
            pltpu.VMEM((T, C), F32),
            pltpu.VMEM((T, C), F32),
            pltpu.VMEM((T, C), F32),
            pltpu.VMEM((T, C), BF),
            pltpu.VMEM((16, C), BF),
            pltpu.VMEM((T, C), F32),
            pltpu.VMEM((T, C), F32),
            pltpu.VMEM((modes, C), F32),
            pltpu.VMEM((modes, C), F32),
            pltpu.VMEM((modes, C), F32),
            pltpu.VMEM((n, modes, C), BF),
            pltpu.VMEM((2, mp, 8, H), F32),
            pltpu.VMEM((H, H), F32),
            pltpu.VMEM((H, 128), F32),
            DMA, DMA, DMA, DMA, DMA, DMA,
            DMA((2, mp)), DMA((2, mp)), DMA((n,)), DMA((n,)),
        ],
        compiler_params=pltpu.CompilerParams(
            collective_id=0, has_side_effects=True, vmem_limit_bytes=40 * 1024 * 1024
        ),
    )(q_mr, k_mr, v_mr, q_li, k_li, short_taps, mr_taps, norm_gain[None], decay_rate, residue, *tables)


def solution(mesh):
    n, mp = mesh.shape["ctx"], mesh.shape["mp"]
    tok = P("ctx", "mp")
    in_specs = (tok,) * 5 + (P(None, None, "mp"), P(None, "mp"), P("mp"), P(None, "mp"), P(None, "mp"))
    return jax.shard_map(
        functools.partial(shards, n, mp), mesh=mesh, in_specs=in_specs, out_specs=(tok, tok), check_vma=False
    )
```

time: 161 us -> 51.9 us (0.32)
  the two profiles are of different devices: /device:TPU:0 before, /device:TPU:31 now
where the time goes in v1:
time: 51.9 us; the launch traced here: 51.1 us
  Pallas kernels  32.1 us (62%)
  local copies, waits for them, and re-layouts  18.4 us (35%)
  between operations  0.67 us (1%)
    pallas_call x1, Pallas kernels, shards(): pl.pallas_call(functools.partial(kernel, n, mp), out_shape=(jax.ShapeDtyp...  32.1 us
    unnamed x38, local copies, waits for them, and re-layouts  18.4 us

profile of v1, /device:TPU:31, one launch (start us, length us, event | category | flops | bytes accessed | tf_op | source)
XLA Modules:
  0.0 51.1 jit_solution(7327780076311322407)
XLA Ops:
  0.6 0.0 copy-start
  0.6 1.0 %copy-done = bf16[256,1024]{1,0:T(8,128)(2,1)S(1)} copy-done((bf16[256,1024]{1,0:T(8,128)(2,1)S(1)}, bf16[256,1024]{1,0:T(8,128)(2,1)}, u32[]{:S(2)}) %copy-start) | copy-done | bytes 524312
  1.7 0.0 copy-start.1
  1.7 1.0 %copy-done.1 = bf16[256,1024]{1,0:T(8,128)(2,1)S(1)} copy-done((bf16[256,1024]{1,0:T(8,128)(2,1)S(1)}, bf16[256,1024]{1,0:T(8,128)(2,1)}, u32[]{:S(2)}) %copy-start.1) | copy-done | bytes 524312
  2.7 0.0 copy-start.2
  2.7 1.0 %copy-done.2 = bf16[256,1024]{1,0:T(8,128)(2,1)S(1)} copy-done((bf16[256,1024]{1,0:T(8,128)(2,1)S(1)}, bf16[256,1024]{1,0:T(8,128)(2,1)}, u32[]{:S(2)}) %copy-start.2) | copy-done | bytes 524312
  3.8 1.0 %copy-done.3 = bf16[256,1024]{1,0:T(8,128)(2,1)S(1)} copy-done((bf16[256,1024]{1,0:T(8,128)(2,1)S(1)}, bf16[256,1024]{1,0:T(8,128)(2,1)}, u32[]{:S(2)}) %copy-start.3) | copy-done | bytes 524312
  4.8 1.0 %copy-done.4 = bf16[256,1024]{1,0:T(8,128)(2,1)S(1)} copy-done((bf16[256,1024]{1,0:T(8,128)(2,1)S(1)}, bf16[256,1024]{1,0:T(8,128)(2,1)}, u32[]{:S(2)}) %copy-start.4) | copy-done | bytes 524312
  5.8 1.0 %copy-done.5 = f32[128,1024]{1,0:T(8,128)S(1)} copy-done((f32[128,1024]{1,0:T(8,128)S(1)}, f32[128,1024]{1,0:T(8,128)}, u32[]{:S(2)}) %copy-start.5) | copy-done | bytes 524312
  6.9 0.9 %copy-done.6 = bf16[256,512]{1,0:T(8,128)(2,1)S(1)} copy-done((bf16[256,512]{1,0:T(8,128)(2,1)S(1)}, bf16[256,512]{1,0:T(8,128)(2,1)}, u32[]{:S(2)}) %copy-start.6) | copy-done | bytes 262168
  7.8 0.9 %copy-done.7 = bf16[256,512]{1,0:T(8,128)(2,1)S(1)} copy-done((bf16[256,512]{1,0:T(8,128)(2,1)S(1)}, bf16[256,512]{1,0:T(8,128)(2,1)}, u32[]{:S(2)}) %copy-start.7) | copy-done | bytes 262168
  8.8 0.9 %copy-done.8 = bf16[512,256]{1,0:T(8,128)(2,1)S(1)} copy-done((bf16[512,256]{1,0:T(8,128)(2,1)S(1)}, bf16[512,256]{1,0:T(8,128)(2,1)}, u32[]{:S(2)}) %copy-start.8) | copy-done | bytes 262168
  9.7 0.9 %copy-done.9 = bf16[512,256]{1,0:T(8,128)(2,1)S(1)} copy-done((bf16[512,256]{1,0:T(8,128)(2,1)S(1)}, bf16[512,256]{1,0:T(8,128)(2,1)}, u32[]{:S(2)}) %copy-start.9) | copy-done | bytes 262168
  10.7 0.9 %copy-done.10 = bf16[256,256]{1,0:T(8,128)(2,1)S(1)} copy-done((bf16[256,256]{1,0:T(8,128)(2,1)S(1)}, bf16[256,256]{1,0:T(8,128)(2,1)}, u32[]{:S(2)}) %copy-start.10) | copy-done | bytes 131096
  11.6 0.9 %copy-done.11 = bf16[256,256]{1,0:T(8,128)(2,1)S(1)} copy-done((bf16[256,256]{1,0:T(8,128)(2,1)S(1)}, bf16[256,256]{1,0:T(8,128)(2,1)}, u32[]{:S(2)}) %copy-start.11) | copy-done | bytes 131096
  12.5 0.9 %copy-done.12 = f32[6,3,1024]{2,1,0:T(4,128)S(1)} copy-done((f32[6,3,1024]{2,1,0:T(4,128)S(1)}, f32[6,3,1024]{2,1,0:T(4,128)}, u32[]{:S(2)}) %copy-start.12) | copy-done | bytes 73752
  13.4 0.8 %copy-done.13 = f32[16,1024]{1,0:T(8,128)S(1)} copy-done((f32[16,1024]{1,0:T(8,128)S(1)}, f32[16,1024]{1,0:T(8,128)}, u32[]{:S(2)}) %copy-start.13) | copy-done | bytes 65560
  14.2 0.8 %copy-done.14 = f32[16,1024]{1,0:T(8,128)S(1)} copy-done((f32[16,1024]{1,0:T(8,128)S(1)}, f32[16,1024]{1,0:T(8,128)}, u32[]{:S(2)}) %copy-start.14) | copy-done | bytes 65560
  15.1 0.8 %copy-done.15 = bf16[128,256]{1,0:T(8,128)(2,1)S(1)} copy-done((bf16[128,256]{1,0:T(8,128)(2,1)S(1)}, bf16[128,256]{1,0:T(8,128)(2,1)}, u32[]{:S(2)}) %copy-start.15) | copy-done | bytes 65560
  15.9 0.8 %copy-done.16 = bf16[128,256]{1,0:T(8,128)(2,1)S(1)} copy-done((bf16[128,256]{1,0:T(8,128)(2,1)S(1)}, bf16[128,256]{1,0:T(8,128)(2,1)}, u32[]{:S(2)}) %copy-start.16) | copy-done | bytes 65560
  16.8 0.7 %copy-done.17 = f32[1024]{0:T(1024)S(1)} copy-done((f32[1024]{0:T(1024)S(1)}, f32[1024]{0:T(1024)}, u32[]{:S(2)}) %copy-start.17) | copy-done | bytes 4120
  17.4 32.1 %shard_map.185 = (bf16[256,1024]{1,0:T(8,128)(2,1)S(1)}, bf16[256,1024]{1,0:T(8,128)(2,1)S(1)}) custom-call(bf16[256,1024]{1,0:T(8,128)(2,1)S(1)} %copy-done, bf16[256,1024]{1,0:T(8,128)(2,1)S(1)} %copy-done.1, bf16[256,1024]{1,0:T(8,128)(2,1)S(1)} %copy-done.2, bf16[256,1024]{1,0:T(8,128)(2,1)S(1)} %copy-done.3, bf16[256,1024]{1,0:T(8,128)(2,1)S(1)} %copy-done.4, ...), custom_call_target="tpu_custom_call" | custom-call | tf_op jit(solution)/shard_map/pallas_call | solution.py:400
  49.5 0.8 %copy.22 = bf16[256,1024]{1,0:T(8,128)(2,1)} copy(bf16[256,1024]{1,0:T(8,128)(2,1)S(1)} %get-tuple-element.4) | data formatting | bytes 1048576
  50.3 0.8 %copy.23 = bf16[256,1024]{1,0:T(8,128)(2,1)} copy(bf16[256,1024]{1,0:T(8,128)(2,1)S(1)} %get-tuple-element.5) | data formatting | bytes 1048576
  (15 shorter events, 0.0 us)
Async XLA Ops:
  0.6 1.0 %copy-start = (bf16[256,1024]{1,0:T(8,128)(2,1)S(1)}, bf16[256,1024]{1,0:T(8,128)(2,1)}, u32[]{:S(2)}) copy-start(bf16[256,1024]{1,0:T(8,128)(2,1)} %q_mr.1) | copy-start | bytes 1572868
  1.7 1.0 %copy-start.1 = (bf16[256,1024]{1,0:T(8,128)(2,1)S(1)}, bf16[256,1024]{1,0:T(8,128)(2,1)}, u32[]{:S(2)}) copy-start(bf16[256,1024]{1,0:T(8,128)(2,1)} %k_mr.1) | copy-start | bytes 1572868
  2.7 1.0 %copy-start.2 = (bf16[256,1024]{1,0:T(8,128)(2,1)S(1)}, bf16[256,1024]{1,0:T(8,128)(2,1)}, u32[]{:S(2)}) copy-start(bf16[256,1024]{1,0:T(8,128)(2,1)} %v_mr.1) | copy-start | bytes 1572868
  3.8 1.0 %copy-start.3 = (bf16[256,1024]{1,0:T(8,128)(2,1)S(1)}, bf16[256,1024]{1,0:T(8,128)(2,1)}, u32[]{:S(2)}) copy-start(bf16[256,1024]{1,0:T(8,128)(2,1)} %q_li.1) | copy-start | bytes 1572868
  4.8 1.0 %copy-start.4 = (bf16[256,1024]{1,0:T(8,128)(2,1)S(1)}, bf16[256,1024]{1,0:T(8,128)(2,1)}, u32[]{:S(2)}) copy-start(bf16[256,1024]{1,0:T(8,128)(2,1)} %k_li.1) | copy-start | bytes 1572868
  5.8 1.0 %copy-start.5 = (f32[128,1024]{1,0:T(8,128)S(1)}, f32[128,1024]{1,0:T(8,128)}, u32[]{:S(2)}) copy-start(f32[128,1024]{1,0:T(8,128)} %mr_taps.1) | copy-start | bytes 1572868
  6.9 0.9 %copy-start.6 = (bf16[256,512]{1,0:T(8,128)(2,1)S(1)}, bf16[256,512]{1,0:T(8,128)(2,1)}, u32[]{:S(2)}) copy-start(bf16[256,512]{1,0:T(8,128)(2,1)} %constant.23.clone.g2l) | copy-start | bytes 786436
  7.8 0.9 %copy-start.7 = (bf16[256,512]{1,0:T(8,128)(2,1)S(1)}, bf16[256,512]{1,0:T(8,128)(2,1)}, u32[]{:S(2)}) copy-start(bf16[256,512]{1,0:T(8,128)(2,1)} %constant.22.clone.g2h) | copy-start | bytes 786436
  8.8 0.9 %copy-start.8 = (bf16[512,256]{1,0:T(8,128)(2,1)S(1)}, bf16[512,256]{1,0:T(8,128)(2,1)}, u32[]{:S(2)}) copy-start(bf16[512,256]{1,0:T(8,128)(2,1)} %constant.21.clone.f2l) | copy-start | bytes 786436
  9.7 0.9 %copy-start.9 = (bf16[512,256]{1,0:T(8,128)(2,1)S(1)}, bf16[512,256]{1,0:T(8,128)(2,1)}, u32[]{:S(2)}) copy-start(bf16[512,256]{1,0:T(8,128)(2,1)} %constant.20.clone.f2h) | copy-start | bytes 786436
  10.7 0.9 %copy-start.10 = (bf16[256,256]{1,0:T(8,128)(2,1)S(1)}, bf16[256,256]{1,0:T(8,128)(2,1)}, u32[]{:S(2)}) copy-start(bf16[256,256]{1,0:T(8,128)(2,1)} %constant.17.clone.f1l) | copy-start | bytes 393220
  11.6 0.9 %copy-start.11 = (bf16[256,256]{1,0:T(8,128)(2,1)S(1)}, bf16[256,256]{1,0:T(8,128)(2,1)}, u32[]{:S(2)}) copy-start(bf16[256,256]{1,0:T(8,128)(2,1)} %constant.16.clone.f1h) | copy-start | bytes 393220
  12.5 0.9 %copy-start.12 = (f32[6,3,1024]{2,1,0:T(4,128)S(1)}, f32[6,3,1024]{2,1,0:T(4,128)}, u32[]{:S(2)}) copy-start(f32[6,3,1024]{2,1,0:T(4,128)} %short.1) | copy-start | bytes 221188
  13.4 0.8 %copy-start.13 = (f32[16,1024]{1,0:T(8,128)S(1)}, f32[16,1024]{1,0:T(8,128)}, u32[]{:S(2)}) copy-start(f32[16,1024]{1,0:T(8,128)} %rate.1) | copy-start | bytes 196612
  14.2 0.8 %copy-start.14 = (f32[16,1024]{1,0:T(8,128)S(1)}, f32[16,1024]{1,0:T(8,128)}, u32[]{:S(2)}) copy-start(f32[16,1024]{1,0:T(8,128)} %res.1) | copy-start | bytes 196612
  15.1 0.8 %copy-start.15 = (bf16[128,256]{1,0:T(8,128)(2,1)S(1)}, bf16[128,256]{1,0:T(8,128)(2,1)}, u32[]{:S(2)}) copy-start(bf16[128,256]{1,0:T(8,128)(2,1)} %constant.19.clone.g1l) | copy-start | bytes 196612
  15.9 0.8 %copy-start.16 = (bf16[128,256]{1,0:T(8,128)(2,1)S(1)}, bf16[128,256]{1,0:T(8,128)(2,1)}, u32[]{:S(2)}) copy-start(bf16[128,256]{1,0:T(8,128)(2,1)} %constant.18.clone.g1h) | copy-start | bytes 196612
  16.8 0.7 %copy-start.17 = (f32[1024]{0:T(1024)S(1)}, f32[1024]{0:T(1024)}, u32[]{:S(2)}) copy-start(f32[1024]{0:T(1024)} %param.25) | copy-start | bytes 12292

commit v2 on v1

--- a/solution.py
+++ b/solution.py
@@ -10,6 +10,8 @@
 
 MESH = pl.DeviceIdType.MESH
 BF = jnp.bfloat16
+IN = 15
+ORDER = (1, 2, 5, 0, 3, 4, 6, 10, 11, 12, 13, 8, 9, 7, 14)
 F32 = jnp.float32
 
 
@@ -72,11 +74,23 @@
 
 
 def kernel(
-    n, mp, q_mr, k_mr, v_mr, q_li, k_li, short, mr_taps, gain, rate, res, f1h, f1l, g1h, g1l, f2h, f2l, g2h, g2l,
-    out_mr, out_li,
-    u_own, u_halo, pack, rims, spec1, spec2, hbuf, lkb, lqb, nbuf, nrim, u32, ylong, wgt, ebuf, carry, st, ss, scale, acc_ss,
-    rim_s, rim_r, halo_s, halo_r, nr_s, nr_r, ss_s, ss_r, st_s, st_r,
+    n, mp, *refs,
 ):
+    ins, refs = refs[:IN], refs[IN:]
+    (out_mr, out_li), refs = refs[:2], refs[2:]
+    vins, refs = refs[:IN], refs[IN:]
+    q_mr, k_mr, v_mr, q_li, k_li, short, mr_taps, gain, rate, res, f1h, f1l, g1h, g1l, fcat = vins
+    (load_s,
+    u_own, u_halo, pack, rims, spec1, spec2, hbuf, lkb, lqb, nbuf, nrim, u32, ylong, wgt, ebuf, emid, late, carry, st, ss, scale, acc_ss,
+    rim_s, rim_r, halo_s, halo_r, nr_s, nr_r, ss_s, ss_r, st_s, st_r) = refs
+    loads = [pltpu.make_async_copy(a, b, load_s.at[i]) for i, (a, b) in enumerate(zip(ins, vins))]
+    for i in ORDER:
+        loads[i].start()
+
+    def need(*which):
+        for i in which:
+            loads[i].wait()
+
     T, C = q_mr.shape
     H = T // 2
     modes = rate.shape[0]
@@ -122,6 +136,7 @@
                 second = jnp.where(here, moved, second)
         pack[:, cols] = jnp.concatenate([first, second], axis=0).astype(BF)
 
+    need(0, 1, 2, 3, 4, 5)
     loop(chunks, pack_body)
 
     @pl.when(jnp.logical_not(not_first))
@@ -162,8 +177,9 @@
 
     def mr_spec(i):
         cols = cols_of(i)
-        store_spectrum(spec1, dot3(f1h[:, 0:H], f1l[:, 0:H], mr_taps[:, cols]), T // 2, cols)
-
+        store_spectrum(spec1, dot3(f1h[:, 0:H], f1l[:, 0:H], mr_taps[:, cols]), H, cols)
+
+    need(6, 10, 11)
     loop(chunks, mr_spec)
 
     @pl.when(not_first)
@@ -185,7 +201,7 @@
     def mr_half(part):
         acc_ss[...] = jnp.zeros(acc_ss.shape, F32)
 
-        def body(i):
+        def mr_body(i):
             cols = cols_of(i)
             if part == 1:
                 win = u_own[:, cols]
@@ -201,7 +217,7 @@
             w = w * w
             acc_ss[...] += w[:, 0:128] + w[:, 128:256]
 
-        loop(chunks, body)
+        loop(chunks, mr_body)
         row = jnp.sum(acc_ss[...].T, axis=0, keepdims=True)
         ss[part, mpi] = jnp.broadcast_to(row, (8, H))
 
@@ -224,15 +240,16 @@
         sc = lax.rsqrt(total / (C * mp) + 1e-06)
         scale[...] = jnp.broadcast_to(sc[0:1], (H, H)).T
 
-        def body(i):
+        def norm_body(i):
             cols = cols_of(i)
             s = scale[...]
             s = jnp.concatenate([s, s], axis=1)
             m = out_mr[part * H : part * H + H, cols].astype(F32)
             nbuf[part * H : part * H + H, cols] = (m * s * gain[0:1, cols]).astype(BF)
 
-        loop(chunks, body)
-
+        loop(chunks, norm_body)
+
+    need(12, 13)
     mr_half(1)
     ss_send(1)
 
@@ -243,6 +260,7 @@
 
     loop(chunks, li_gates)
 
+    need(7, 8, 9, 14)
     norm_half(1)
 
     @pl.when(not_last)
@@ -275,13 +293,13 @@
             hbuf[pl.ds(pl.multiple_of(k * 8, 8), 8), cols] = tree(g)
             return tuple(a * b for a, b in zip(g, d8))
 
-        lax.fori_loop(0, T // 8, step, g, unroll=4)
+        lax.fori_loop(0, H // 8, step, g, unroll=4)
 
     loop(C // 128, h_group)
 
     def li_spec(i):
         cols = cols_of(i)
-        store_spectrum(spec2, dot3(f2h[...], f2l[...], hbuf[:, cols]), T, cols)
+        store_spectrum(spec2, dot3(f1h[:, 0:H], f1l[:, 0:H], hbuf[:, cols]), H, cols)
 
     loop(chunks, li_spec)
 
@@ -291,6 +309,34 @@
 
     mr_half(0)
     ss_send(0)
+
+    E = H + 16
+
+    def li_u_late(i):
+        cols = cols_of(i)
+        lv = conv3(nbuf[E:T, cols].astype(F32), nbuf[H:E, cols].astype(F32)[8:], short[5, :, cols])
+        u32[E:T, cols] = (lkb[E:T, cols] * lv).astype(BF).astype(F32)
+
+    loop(chunks, li_u_late)
+
+    def horner(lo, hi, acc, d8, cols):
+        def step(k, acc):
+            u = u32[pl.ds(pl.multiple_of(k * 8, 8), 8), cols]
+            return tuple(a * d + u for a, d in zip(acc, d8))
+
+        return lax.fori_loop(lo // 8, hi // 8, step, acc, unroll=2)
+
+    def zeros8():
+        return tuple(jnp.zeros((8, 128), F32) for _ in range(modes))
+
+    def ends_late(i):
+        cols = cols_of(i, 128)
+        d8 = [jnp.exp(-8.0 * a) for a in rows_of(rate, cols)]
+        acc = horner(E, T, zeros8(), d8, cols)
+        for m in range(modes):
+            late[8 * m : 8 * m + 8, cols] = acc[m]
+
+    loop(C // 128, ends_late)
     norm_half(0)
 
     @pl.when(not_first)
@@ -299,8 +345,8 @@
 
     def li_u(i):
         cols = cols_of(i)
-        lv = conv3(nbuf[:, cols].astype(F32), nrim[:, cols].astype(F32)[8:], short[5, :, cols])
-        u32[:, cols] = (lkb[:, cols] * lv).astype(BF).astype(F32)
+        lv = conv3(nbuf[0:E, cols].astype(F32), nrim[:, cols].astype(F32)[8:], short[5, :, cols])
+        u32[0:E, cols] = (lkb[0:E, cols] * lv).astype(BF).astype(F32)
 
     loop(chunks, li_u)
 
@@ -308,14 +354,14 @@
         cols = cols_of(i, 128)
         r = rows_of(rate, cols)
         d8 = [jnp.exp(-8.0 * a) for a in r]
-
-        def step(k, acc):
-            u = u32[pl.ds(pl.multiple_of(k * 8, 8), 8), cols]
-            return tuple(a * d + u for a, d in zip(acc, d8))
-
-        acc = lax.fori_loop(0, T // 8, step, tuple(jnp.zeros((8, 128), F32) for _ in r), unroll=4)
+        place = [jnp.exp(-a * (7.0 - sub)) for a in r]
+        acc = horner(0, H, zeros8(), d8, cols)
         for m in range(modes):
-            ebuf[m : m + 1, cols] = jnp.sum(acc[m] * jnp.exp(-r[m] * (7.0 - sub)), axis=0, keepdims=True)
+            emid[m : m + 1, cols] = jnp.sum(acc[m] * place[m], axis=0, keepdims=True)
+        acc = horner(H, E, acc, d8, cols)
+        for m in range(modes):
+            whole = acc[m] * jnp.exp(-float(T - E) * r[m]) + late[8 * m : 8 * m + 8, cols]
+            ebuf[m : m + 1, cols] = jnp.sum(whole * place[m], axis=0, keepdims=True)
 
     loop(C // 128, ends_group)
     st[ctx] = ebuf[...].astype(BF)
@@ -333,9 +379,13 @@
 
     def li_local(i):
         cols = cols_of(i)
-        win = u32[:, cols].astype(BF)
-        u = dot(f2h[...], win) + dot(f2l[...], win)
-        ylong[:, cols] = dot3(g2h[...], g2l[...], spectrum_product(u, spec2[:, cols], T))
+        win = jnp.concatenate([u32[0:H, cols], u32[H:T, cols]], axis=1).astype(BF)
+        u = dot(fcat[...], jnp.concatenate([win, win], axis=0))
+        spec = spec2[:, cols]
+        p = spectrum_product(u, jnp.concatenate([spec, spec], axis=1), H)
+        y = dot3(g1h[...], g1l[...], p)
+        ylong[0:H, cols] = y[:, :CW]
+        ylong[H:T, cols] = y[:, CW:]
 
     loop(chunks, li_local)
 
@@ -354,7 +404,7 @@
         w = rows_of(wgt, cols)
         s = rows_of(carry, cols)
         d8 = [jnp.exp(-8.0 * a) for a in r]
-        g = tuple(b * c * jnp.exp(-a * (sub + 1.0)) for a, b, c in zip(r, w, s))
+        start = [b * jnp.exp(-a * (sub + 1.0)) for a, b in zip(r, w)]
 
         def step(k, g):
             rows = pl.ds(pl.multiple_of(k * 16, 16), 16)
@@ -366,7 +416,10 @@
             out_li[rows, cols] = (lqb[rows, cols] * y.astype(BF).astype(F32)).astype(BF)
             return g
 
-        lax.fori_loop(0, T // 16, step, g, unroll=2)
+        lax.fori_loop(0, H // 16, step, tuple(a * b for a, b in zip(start, s)), unroll=2)
+        mid = rows_of(emid, cols)
+        s = [a * jnp.exp(-float(H) * b) + c for a, b, c in zip(s, r, mid)]
+        lax.fori_loop(H // 16, T // 16, step, tuple(a * b for a, b in zip(start, s)), unroll=2)
 
     loop(C // 128, out_group)
 
@@ -391,25 +444,27 @@
     T, C = q_mr.shape
     modes = decay_rate.shape[0]
     (f1h, f1l), (g1h, g1l) = dft_tables(T, T // 2, T)
-    (f2h, f2l), (g2h, g2l) = dft_tables(2 * T, 0, T)
-    g2h, g2l = g2h[:T], g2l[:T]
-    tables = [jnp.asarray(a) for a in (f1h, f1l, g1h, g1l, f2h, f2l, g2h, g2l)]
+    fcat = np.concatenate([f1h[:, T // 2 :], f1l[:, T // 2 :]], axis=1)
+    args = [q_mr, k_mr, v_mr, q_li, k_li, short_taps, mr_taps, norm_gain[None], decay_rate, residue]
+    args += [jnp.asarray(a) for a in (f1h, f1l, g1h, g1l, fcat)]
     vm = pl.BlockSpec(memory_space=pltpu.VMEM)
     DMA = pltpu.SemaphoreType.DMA
     H = T // 2
     return pl.pallas_call(
         functools.partial(kernel, n, mp),
         out_shape=(jax.ShapeDtypeStruct((T, C), BF), jax.ShapeDtypeStruct((T, C), BF)),
-        in_specs=[vm] * 18,
+        in_specs=[pl.BlockSpec(memory_space=pltpu.HBM)] * IN,
         out_specs=(vm, vm),
-        scratch_shapes=[
+        scratch_shapes=[pltpu.VMEM(a.shape, a.dtype) for a in args]
+        + [
+            DMA((IN,)),
             pltpu.VMEM((T, C), BF),
             pltpu.VMEM((H, C), BF),
             pltpu.VMEM((16, C), BF),
             pltpu.VMEM((16, C), BF),
             pltpu.VMEM((T + 8, C), F32),
-            pltpu.VMEM((2 * T + 8, C), F32),
-            pltpu.VMEM((T, C), F32),
+            pltpu.VMEM((T + 8, C), F32),
+            pltpu.VMEM((H, C), F32),
             pltpu.VMEM((T, C), F32),
             pltpu.VMEM((T, C), F32),
             pltpu.VMEM((T, C), BF),
@@ -419,6 +474,8 @@
             pltpu.VMEM((modes, C), F32),
             pltpu.VMEM((modes, C), F32),
             pltpu.VMEM((modes, C), F32),
+            pltpu.VMEM((8 * modes, C), F32),
+            pltpu.VMEM((modes, C), F32),
             pltpu.VMEM((n, modes, C), BF),
             pltpu.VMEM((2, mp, 8, H), F32),
             pltpu.VMEM((H, H), F32),
@@ -427,9 +484,9 @@
             DMA((2, mp)), DMA((2, mp)), DMA((n,)), DMA((n,)),
         ],
         compiler_params=pltpu.CompilerParams(
-            collective_id=0, has_side_effects=True, vmem_limit_bytes=40 * 1024 * 1024
+            collective_id=0, has_side_effects=True, vmem_limit_bytes=56 * 1024 * 1024
         ),
-    )(q_mr, k_mr, v_mr, q_li, k_li, short_taps, mr_taps, norm_gain[None], decay_rate, residue, *tables)
+    )(*args)
 
 
 def solution(mesh):

time: 51.9 us -> 35.3 us (0.68); the launches traced: 51.1 us -> 35.1 us
  local copies, waits for them, and re-layouts: 18.4 us -> 2.72 us
    unnamed x38 -> x4, local copies, waits for them, and re-layouts: 18.4 us -> 2.72 us
where the time goes in v2:
time: 35.3 us; the launch traced here: 35.1 us
  Pallas kernels  31.8 us (90%)
  local copies, waits for them, and re-layouts  2.72 us (8%)
  between operations  0.65 us (2%)
    pallas_call x1, Pallas kernels, shards(): pl.pallas_call(functools.partial(kernel, n, mp), out_shape=(jax.ShapeDtyp...  31.8 us
    unnamed x4, local copies, waits for them, and re-layouts  2.72 us

profile of v2, /device:TPU:31, one launch (start us, length us, event | category | flops | bytes accessed | tf_op | source)
XLA Modules:
  0.0 35.1 jit_solution(2821721966735523298)
XLA Ops:
  0.6 31.8 %shard_map.158 = (bf16[256,1024]{1,0:T(8,128)(2,1)}, bf16[256,1024]{1,0:T(8,128)(2,1)}) custom-call(bf16[256,1024]{1,0:T(8,128)(2,1)} %refs_0_.1, bf16[256,1024]{1,0:T(8,128)(2,1)} %refs_1_.1, bf16[256,1024]{1,0:T(8,128)(2,1)} %refs_2_.1, bf16[256,1024]{1,0:T(8,128)(2,1)} %refs_3_.1, bf16[256,1024]{1,0:T(8,128)(2,1)} %refs_4_.1, f32[6,3,1024]{2,1,0:T(4,128)} %refs_5_.1, ...), custom_call_target="tpu_custom_call" | custom-call | tf_op jit(solution)/shard_map/pallas_call | solution.py:453
  32.4 0.0 copy-start
  32.4 1.9 %copy.19 = bf16[256,1024]{1,0:T(8,128)(2,1)} copy(bf16[256,1024]{1,0:T(8,128)(2,1)} %get-tuple-element.4) | data formatting | bytes 1048576
  34.4 0.0 copy-done
  34.4 0.8 %copy.20 = bf16[256,1024]{1,0:T(8,128)(2,1)} copy(bf16[256,1024]{1,0:T(8,128)(2,1)S(1)} %copy-done) | data formatting | bytes 1048576
Async XLA Ops:
  32.4 1.9 %copy-start = (bf16[256,1024]{1,0:T(8,128)(2,1)S(1)}, bf16[256,1024]{1,0:T(8,128)(2,1)}, u32[]{:S(2)}) copy-start(bf16[256,1024]{1,0:T(8,128)(2,1)} %get-tuple-element.5) | copy-start | bytes 1572868
